TPU v7x, 32 devices: a whole 2x2x4 slice. The times are simulated.
32 devices in a mesh: expert: 4 (over z), mp: 8 (over y, x, core).
Axes of the slice: x: 2, y: 2, z: 4, core: 2. Of those that a mesh axis runs over, the one named last changes fastest.
Arguments:
- tokens: bfloat16 [2048, 2048], P('expert', 'mp'), may hold values from -6 to 6
- expert_route: int32 [2048, 2], P('expert'), may hold values from 0 to 3, all different within a row; in each aligned block of 512 rows (0 to 511, 512 to 1023, ...) at most 512 rows name the same one
- route_gate: float32 [2048, 2], P('expert'), may hold values from 0.05 to 1
- request_lengths: int32 [16], replicated, may hold values from 1 to 1024, 2048 in all
- request_adapter: int32 [16], replicated, may hold values from 0 to 63, as said below
- request_order: int32 [16], replicated, may hold values from 0 to 15, each once
- gate_weight: bfloat16 [4, 5632, 2048], P('expert', 'mp'), may hold values from -0.125 to 0.125
- up_weight: bfloat16 [4, 5632, 2048], P('expert', 'mp'), may hold values from -0.125 to 0.125
- down_weight: bfloat16 [4, 5632, 2048], P('expert', 'mp'), may hold values from -0.109375 to 0.109375
- adapter_in: bfloat16 [4, 1024, 2048], P('expert', 'mp'), may hold values from -0.125 to 0.125
- adapter_out: bfloat16 [4, 5632, 1024], P('expert', 'mp'), may hold values from -1.5 to 1.5
Outputs:
- mixed: bfloat16 [2048, 2048], P('expert', 'mp')
Inputs may be any that keep to these rules, and one draw needn't show every extreme that they name: `expert_route`: the two entries of a row differ; within each aligned block of 512 rows (the tokens held at one position along `expert`) no expert is named by more than 512 rows, and in some block some expert is named by exactly 512 rows. `request_lengths`: they sum to 2048; the largest is 1024. `request_order`: each request index appears once. `request_adapter`: exactly 16 different adapters appear.
All inputs are finite; a program needn't handle non-finite values.
Results may differ from a plain program's by a relative error of at most 0.035.
Values may be sent and summed in bfloat16 or wider, within the bound.
A program may use at most 64 MiB of HBM per device.

v0:
```python
import jax
import jax.numpy as jnp
from jax import lax
from jax.sharding import PartitionSpec as P

RANK = 16
ADAPTERS = 64


def token_adapters(request_lengths, request_adapter, request_order, first_token, token_count):
    request_ids = jnp.arange(request_lengths.shape[0], dtype=jnp.int32)
    chosen = (request_order[:, None] == request_ids[None, :]).astype(jnp.int32)
    packed_lengths = jnp.sum(chosen * request_lengths[None, :], axis=1, dtype=jnp.int32)
    packed_adapters = jnp.sum(chosen * request_adapter[None, :], axis=1, dtype=jnp.int32)
    boundary = jnp.cumsum(packed_lengths, dtype=jnp.int32)
    positions = first_token + jnp.arange(token_count, dtype=jnp.int32)
    packed_index = jnp.sum(
        (boundary[None, :] <= positions[:, None]).astype(jnp.int32), axis=1, dtype=jnp.int32
    )
    matches = (packed_index[:, None] == request_ids[None, :]).astype(jnp.int32)
    return jnp.sum(matches * packed_adapters[None, :], axis=1, dtype=jnp.int32)


def expert_slots(routes, groups, capacity):
    flat_routes = routes.reshape(-1)
    one_hot = (flat_routes[:, None] == jnp.arange(groups, dtype=jnp.int32)[None, :]).astype(
        jnp.int32
    )
    before = jnp.cumsum(one_hot, axis=0, dtype=jnp.int32) - one_hot
    seat_index = jnp.sum(before * one_hot, axis=1, dtype=jnp.int32)
    return (flat_routes * capacity + seat_index).reshape(routes.shape)


def contract_last(left, right):
    return lax.dot_general(
        left, right, (((1,), (1,)), ((), ())), preferred_element_type=jnp.float32
    )


def on_device(
    tokens,
    expert_route,
    route_gate,
    request_lengths,
    request_adapter,
    request_order,
    gate_weight,
    up_weight,
    down_weight,
    adapter_in,
    adapter_out,
):
    tok_rows = tokens.shape[0]
    groups = lax.axis_size("expert")
    capacity = 4 * tok_rows // groups
    total_slots = groups * capacity
    source_group = lax.axis_index("expert")
    adapter_of = token_adapters(
        request_lengths, request_adapter, request_order, source_group * tok_rows, tok_rows
    )
    slot_index = expert_slots(expert_route, groups, capacity)
    flat_slots = slot_index.reshape(-1)
    flat_tokens = jnp.broadcast_to(
        jnp.arange(tok_rows, dtype=jnp.int32)[:, None], slot_index.shape
    ).reshape(-1)
    slot_token = jnp.zeros((total_slots,), jnp.int32).at[flat_slots].set(flat_tokens)
    filled = jnp.zeros((total_slots,), jnp.bool_).at[flat_slots].set(True)
    slot_adapter = jnp.where(filled, adapter_of[slot_token], -1)
    gate_w = gate_weight[0]
    up_w = up_weight[0]
    rank_w = adapter_in[0]
    blank = jnp.zeros((), tokens.dtype)
    full_rows = lax.all_gather(tokens, "mp", axis=1, tiled=True)
    send_rows = jnp.where(filled[:, None], full_rows[slot_token], blank)
    arrived, arrived_adapter = (
        lax.all_to_all(send_rows, "expert", split_axis=0, concat_axis=0, tiled=True),
        lax.all_to_all(slot_adapter, "expert", split_axis=0, concat_axis=0, tiled=True),
    )
    gate_pre = contract_last(arrived, gate_w)
    up_base = contract_last(arrived, up_w)
    rank_cols = contract_last(arrived, rank_w)
    row_count = arrived.shape[0]
    per_device = rank_w.shape[0] // RANK
    local_adapter = arrived_adapter - lax.axis_index("mp") * per_device
    local_pick = (
        local_adapter[:, None] == jnp.arange(per_device, dtype=jnp.int32)[None, :]
    ).astype(jnp.float32)
    rank_part = jnp.sum(
        rank_cols.reshape(row_count, per_device, RANK) * local_pick[:, :, None], axis=1
    )
    rank = lax.psum(rank_part.astype(jnp.bfloat16), "mp")
    chosen = (arrived_adapter[:, None] == jnp.arange(ADAPTERS, dtype=jnp.int32)[None, :]).astype(
        jnp.bfloat16
    )
    expanded = (rank[:, None, :] * chosen[:, :, None]).reshape(row_count, ADAPTERS * RANK)
    up = up_base + contract_last(expanded, adapter_out[0])
    hidden = (jax.nn.silu(gate_pre) * up).astype(jnp.bfloat16)
    down_w = down_weight[0]
    scattered = lax.psum_scatter(
        lax.dot_general(
            down_w, hidden, (((0,), (1,)), ((), ())), preferred_element_type=jnp.float32
        ).astype(jnp.bfloat16),
        "mp",
        scatter_dimension=0,
        tiled=True,
    )
    returned = lax.all_to_all(scattered, "expert", split_axis=1, concat_axis=1, tiled=True)
    returned_rows = jnp.transpose(returned)
    picked = returned_rows[slot_index].astype(jnp.float32)
    mixed = jnp.sum(route_gate[:, :, None] * picked, axis=1)
    return mixed.astype(jnp.bfloat16)


def solution(mesh):
    in_specs = (
        P("expert", "mp"),
        P("expert", None),
        P("expert", None),
        P(),
        P(),
        P(),
        P("expert", "mp", None),
        P("expert", "mp", None),
        P("expert", "mp", None),
        P("expert", "mp", None),
        P("expert", "mp", None),
    )
    out_specs = P("expert", "mp")
    return jax.shard_map(
        on_device, mesh=mesh, in_specs=in_specs, out_specs=out_specs, check_vma=False
    )
```

profile of v0, /device:TPU:0, one launch (start us, length us, event | category | flops | bytes accessed | tf_op | source)
XLA Modules:
  0.0 456.2 jit_solution(7238121356525590581)
XLA Ops:
  6.5 0.0 copy-start
  6.5 0.0 all-gather.2.cloned.1.call-start
  6.5 0.7 all-gather.2.cloned.1.call-update
  7.3 1.0 copy.26
  8.2 0.2 eq.89
  8.4 0.2 eq.85
  8.6 1.1 reduce-window.18
  9.7 0.2 slice_reduce_fusion
  10.0 0.2 reduce-window.19
  10.1 0.1 add_bitcast_fusion
  10.2 0.9 reduce_sum.74
  11.1 1.7 compare_select_fusion
  12.8 1.1 mul.99
  14.0 0.2 reshape.207
  14.2 0.9 select_reduce_fusion.2
  15.0 0.1 copy.29
  15.2 0.1 reduce.1
  15.3 4.3 scatter_custom_fusion.1
  19.6 0.1 convert_reduce_fusion
  19.7 0.1 select_reduce_fusion
  19.8 13.2 %gather_fusion.1 = s32[2048]{0:T(1024)S(1)} fusion(s32[512]{0:T(512)S(1)} %select_reduce_fusion, s32[2048]{0:T(1024)S(1)} %fusion.14), kind=kCustom, calls=%fused_computation.1 | custom fusion | bytes 24576 | tf_op jit(solution)/shard_map/gather | solution.py:68
  33.0 4.3 scatter_custom_fusion
  37.4 0.6 broadcast_select_fusion.1
  38.0 6.3 %all-to-all-start.1 = ((s32[4,512,1]{1,2,0:T(1,128)}), s32[4,512,1]{1,2,0:T(1,128)S(1)}, u32[]{:S(2)}, u32[]{:S(2)}) async-start(s32[4,512,1]{1,2,0:T(1,128)} %bitcast.10), calls=%async_computation.1 | async-start | bytes 16384 | tf_op jit(solution)/shard_map/all_to_all | solution.py:77
  44.3 0.0 all-gather.2.cloned.1.call-done
  44.4 18.2 %gather_fusion = bf16[2048,2048]{1,0:T(8,128)(2,1)} fusion(bf16[512,2048]{1,0:T(8,128)(2,1)} %all-gather.2.cloned.1.call-done, s32[2048]{0:T(1024)S(1)} %fusion.14), kind=kCustom, calls=%fused_computation | custom fusion | bytes 16785408 | tf_op jit(solution)/shard_map/gather | solution.py:74
  62.5 7.2 %broadcast_select_fusion = bf16[4,512,2048]{2,1,0:T(8,128)(2,1)} fusion(bf16[4,512,2048]{2,1,0:T(8,128)(2,1)} %bitcast.54, pred[4,512]{1,0:T(4,128)(4,1)S(1)} %broadcast_in_dim.26), kind=kLoop, calls=%fused_computation.6 | loop fusion | flops 4194304 | bytes 16779264 | tf_op jit(solution)/shard_map/jit(_where)/select_n | solution.py:74
  69.8 0.0 all-to-all-done.1
  69.8 5.7 %all-to-all-start = ((bf16[4,512,2048]{2,1,0:T(8,128)(2,1)}), bf16[4,512,2048]{2,1,0:T(8,128)(2,1)}, u32[]{:S(2)}, u32[]{:S(2)}) async-start(bf16[4,512,2048]{2,1,0:T(8,128)(2,1)} %broadcast_select_fusion), calls=%async_computation | async-start | bytes 16777216 | tf_op jit(solution)/shard_map/all_to_all | solution.py:76
  75.5 0.0 all-reduce.2.cloned.1.call-start
  75.6 182.9 %all-to-all-done = bf16[4,512,2048]{2,1,0:T(8,128)(2,1)} async-done(((bf16[4,512,2048]{2,1,0:T(8,128)(2,1)}), bf16[4,512,2048]{2,1,0:T(8,128)(2,1)}, u32[]{:S(2)}, u32[]{:S(2)}) %all-to-all-start) | async-done | bytes 8388640 | tf_op jit(solution)/shard_map/all_to_all | solution.py:76
  258.5 7.0 %fusion.7 = bf16[2048,16]{0,1:T(8,128)(2,1)} fusion(bf16[2048,2048,1]{1,0,2:T(8,128)(2,1)} %bitcast.7, bf16[8,16,2048]{2,1,0:T(8,128)(2,1)} %bitcast.64, f32[2048,8]{0,1:T(8,128)S(1)} %fusion.9), kind=kOutput, calls=%fused_computation.16 | convolution fusion | flops 1074233344 | bytes 9043968 | tf_op jit(solution)/shard_map/dot_general | solution.py:35
  265.5 0.0 all-reduce.2.cloned.1.call-update
  265.5 0.2 reduce-scatter.2.cloned.1.call-start
  265.8 0.0 copy-start.2
  265.8 11.2 %fusion.1 = f32[2048,704]{0,1:T(8,128)} fusion(bf16[2048,2048]{1,0:T(8,128)(2,1)} %bitcast.4, bf16[1,704,2048]{2,1,0:T(8,128)(2,1)} %param.18), kind=kOutput, calls=%fused_computation.9 | convolution fusion | flops 5905580032 | bytes 17039360 | tf_op jit(solution)/shard_map/dot_general | solution.py:35
  277.0 0.0 copy-done.2
  277.0 10.1 %fusion.3 = f32[2048,704]{0,1:T(8,128)} fusion(bf16[2048,2048]{1,0:T(8,128)(2,1)} %bitcast.4, bf16[1,704,2048]{2,1,0:T(8,128)(2,1)S(1)} %copy-done.2), kind=kOutput, calls=%fused_computation.11 | convolution fusion | flops 5905580032 | bytes 17039360 | tf_op jit(solution)/shard_map/dot_general | solution.py:35
  287.1 30.2 %all-reduce.2.cloned.1.call-done = bf16[2048,16]{0,1:T(8,128)(2,1)} async-done(((bf16[2048,16]{0,1:T(8,128)(2,1)}), bf16[2048,16]{0,1:T(8,128)(2,1)}) %all-reduce.2.cloned.1.call-update) | async-done | bytes 65552 | tf_op jit(solution)/shard_map/psum | solution.py:91
  317.3 3.2 broadcast_multiply_fusion
  320.5 0.0 copy-done
  320.5 16.9 %convert_bitcast_fusion = bf16[2048,2048]{0,1:T(8,128)(2,1)} fusion(bf16[1,704,2048]{2,1,0:T(8,128)(2,1)S(1)} %copy-done, f32[2048,704]{0,1:T(8,128)} %fusion.1, f32[2048,704]{0,1:T(8,128)} %fusion.3, bf16[2048,1024]{0,1:T(8,128)(2,1)} %bitcast.55, bf16[1,704,1024]{2,1,0:T(8,128)(2,1)} %param.21), kind=kOutput, calls=%fused_computation.5 | convolution fusion | flops 8872656896 | bytes 28442624 | tf_op jit(solution)/shard_map/dot_general | solution.py:100
  337.4 0.0 copy-start.1
  337.4 0.0 reduce-scatter.2.cloned.1.call-update
  337.4 70.9 %reduce-scatter.2.cloned.1.call-done = bf16[256,2048]{0,1:T(8,128)(2,1)} async-done(((bf16[2048,2048]{0,1:T(8,128)(2,1)}), bf16[256,2048]{0,1:T(8,128)(2,1)}) %reduce-scatter.2.cloned.1.call-update) | async-done | bytes 1048592 | tf_op jit(solution)/shard_map/reduce_scatter | solution.py:99
  408.3 4.6 %all-to-all-start.2 = ((bf16[256,4,512]{0,2,1:T(8,128)(2,1)}), bf16[256,4,512]{0,2,1:T(8,128)(2,1)}, u32[]{:S(2)}, u32[]{:S(2)}) async-start(bf16[256,4,512]{0,2,1:T(8,128)(2,1)} %bitcast.56), calls=%async_computation.3 | async-start | bytes 2097152 | tf_op jit(solution)/shard_map/all_to_all | solution.py:107
  412.9 0.2 reshape.189
  413.0 0.0 copy-done.1
  413.0 0.9 copy.25
  413.9 24.8 %all-to-all-done.2 = bf16[256,4,512]{0,2,1:T(8,128)(2,1)} async-done(((bf16[256,4,512]{0,2,1:T(8,128)(2,1)}), bf16[256,4,512]{0,2,1:T(8,128)(2,1)}, u32[]{:S(2)}, u32[]{:S(2)}) %all-to-all-start.2) | async-done | bytes 1048608 | tf_op jit(solution)/shard_map/all_to_all | solution.py:107
  438.7 4.8 %gather_fusion.2 = bf16[1024,256]{1,0:T(8,128)(2,1)S(1)} fusion(bf16[2048,256]{1,0:T(8,128)(2,1)} %bitcast.18, s32[1024]{0:T(1024)S(1)} %broadcast_clamp_fusion), kind=kCustom, calls=%fused_computation.2 | custom fusion | bytes 1052672 | tf_op jit(solution)/shard_map/gather | solution.py:109
  443.5 1.5 reshape.215
  445.0 4.6 %multiply_reduce_fusion = bf16[512,256]{1,0:T(8,128)(2,1)} fusion(f32[512,2,256]{2,1,0:T(2,128)} %reshape.215, f32[512,2]{1,0:T(8,128)} %copy.25), kind=kLoop, calls=%fused_computation.17 | loop fusion | flops 393216 | bytes 1314816 | tf_op jit(solution)/shard_map/reduce_sum | solution.py:110
  (13 shorter events, 0.2 us)
Async XLA Ops:
  6.5 313.9 %copy-start = (bf16[1,704,2048]{2,1,0:T(8,128)(2,1)S(1)}, bf16[1,704,2048]{2,1,0:T(8,128)(2,1)}, u32[]{:S(2)}) copy-start(bf16[1,704,2048]{2,1,0:T(8,128)(2,1)} %param.19) | copy-start | bytes 8650756
  6.5 37.8 %all-gather.2.cloned.1.call-start = ((), (), s32[]{:S(2)}) async-start(), calls=%async_computation.4 | async-start | bytes 2359296 | tf_op jit(solution)/shard_map/all_gather | solution.py:73
  38.0 31.8 %all-to-all-start.1 = ((s32[4,512,1]{1,2,0:T(1,128)}), s32[4,512,1]{1,2,0:T(1,128)S(1)}, u32[]{:S(2)}, u32[]{:S(2)}) async-start(s32[4,512,1]{1,2,0:T(1,128)} %bitcast.10), calls=%async_computation.1 | async-start | bytes 16384 | tf_op jit(solution)/shard_map/all_to_all | solution.py:77
  69.8 188.7 %all-to-all-start = ((bf16[4,512,2048]{2,1,0:T(8,128)(2,1)}), bf16[4,512,2048]{2,1,0:T(8,128)(2,1)}, u32[]{:S(2)}, u32[]{:S(2)}) async-start(bf16[4,512,2048]{2,1,0:T(8,128)(2,1)} %broadcast_select_fusion), calls=%async_computation | async-start | bytes 16777216 | tf_op jit(solution)/shard_map/all_to_all | solution.py:76
  75.5 241.8 %all-reduce.2.cloned.1.call-start = ((), (), s32[]{:S(2)}) async-start(), calls=%async_computation.5 | async-start | bytes 131072 | tf_op jit(solution)/shard_map/psum | solution.py:91
  265.5 142.7 %reduce-scatter.2.cloned.1.call-start = ((), (), s32[]{:S(2)}) async-start(), calls=%async_computation.6 | async-start | bytes 9437184 | tf_op jit(solution)/shard_map/reduce_scatter | solution.py:99
  265.8 11.2 %copy-start.2 = (bf16[1,704,2048]{2,1,0:T(8,128)(2,1)S(1)}, bf16[1,704,2048]{2,1,0:T(8,128)(2,1)}, u32[]{:S(2)}) copy-start(bf16[1,704,2048]{2,1,0:T(8,128)(2,1)} %param.17) | copy-start | bytes 8650756
  337.4 75.7 %copy-start.1 = (f32[512,2]{0,1:T(2,128)S(1)}, f32[512,2]{0,1:T(2,128)}, u32[]{:S(2)}) copy-start(f32[512,2]{0,1:T(2,128)} %param.13) | copy-start | bytes 12292
  408.3 30.4 %all-to-all-start.2 = ((bf16[256,4,512]{0,2,1:T(8,128)(2,1)}), bf16[256,4,512]{0,2,1:T(8,128)(2,1)}, u32[]{:S(2)}, u32[]{:S(2)}) async-start(bf16[256,4,512]{0,2,1:T(8,128)(2,1)} %bitcast.56), calls=%async_computation.3 | async-start | bytes 2097152 | tf_op jit(solution)/shard_map/all_to_all | solution.py:107
Sparse Core Ops, SparseCore 0:
  9.2 30.8 all-gather.1
  265.7 51.5 all-reduce.1
  337.5 70.6 reduce-scatter.1
where the time goes:
time: 457 us; the launch traced here: 456 us
  waiting for transfers between devices  310 us (68%)
  local copies, waits for them, and re-layouts  51.3 us (11%)
  matrix products  45.2 us (10%)
  other arithmetic  20.1 us (4%)
  starting transfers between devices  16.8 us (4%)
  between operations  13.3 us (3%)
    all_to_all x1, waiting for transfers between devices, on_device(): lax.all_to_all(send_rows, 'expert', split_axis=0, concat_axis=0, tiled=True)  183 us
    reduce_scatter x1, waiting for transfers between devices, on_device(): lax.psum_scatter(lax.dot_general(down_w, hidden, (((0,), (1,)), ((), ()))...  70.9 us
    psum x1, waiting for transfers between devices, on_device(): rank = lax.psum(rank_part.astype(jnp.bfloat16), 'mp')  30.2 us
    dot_general x3, matrix products, contract_last(): lax.dot_general(left, right, (((1,), (1,)), ((), ())), preferred_element_...  28.3 us
    all_to_all x1, waiting for transfers between devices, on_device(): lax.all_to_all(scattered, 'expert', split_axis=1, concat_axis=1, tiled=True)  24.8 us
    gather x1, local copies, waits for them, and re-layouts, on_device(): send_rows = jnp.where(filled[:, None], full_rows[slot_token], blank)  18.2 us
    dot_general x1, matrix products, on_device(): lax.dot_general(down_w, hidden, (((0,), (1,)), ((), ())), preferred_eleme...  16.9 us
    gather x1, local copies, waits for them, and re-layouts, on_device(): slot_adapter = jnp.where(filled, adapter_of[slot_token], -1)  13.2 us
  transfers between devices with their start and end apart: 6, of which 4 were waited for; matrix products, arithmetic and copies ran while one was open for 17% of the time, Pallas kernels for 0%

commit v1 on v0

v1 whole, which is shorter than its diff:
```python
import functools

import jax
import jax.numpy as jnp
from jax import lax
from jax.experimental import pallas as pl
from jax.experimental.pallas import tpu as pltpu
from jax.sharding import PartitionSpec as P

RANK = 16
ADAPTERS = 64
MESH = pl.DeviceIdType.MESH


def contract_last(left, right):
    return lax.dot_general(
        left, right, (((1,), (1,)), ((), ())), preferred_element_type=jnp.float32
    )


def token_adapters(request_lengths, request_adapter, request_order, token_count):
    request_ids = jnp.arange(request_lengths.shape[0], dtype=jnp.int32)
    chosen = (request_order[:, None] == request_ids[None, :]).astype(jnp.int32)
    packed_lengths = jnp.sum(chosen * request_lengths[None, :], axis=1, dtype=jnp.int32)
    packed_adapters = jnp.sum(chosen * request_adapter[None, :], axis=1, dtype=jnp.int32)
    boundary = jnp.cumsum(packed_lengths, dtype=jnp.int32)
    positions = jnp.arange(token_count, dtype=jnp.int32)
    packed_index = jnp.sum(
        (boundary[None, :] <= positions[:, None]).astype(jnp.int32), axis=1, dtype=jnp.int32
    )
    matches = (packed_index[:, None] == request_ids[None, :]).astype(jnp.int32)
    return jnp.sum(matches * packed_adapters[None, :], axis=1, dtype=jnp.int32)


def plain(
    tokens,
    expert_route,
    route_gate,
    request_lengths,
    request_adapter,
    request_order,
    gate_weight,
    up_weight,
    down_weight,
    adapter_in,
    adapter_out,
):
    groups = lax.axis_size("expert")
    tok_rows, cols = tokens.shape
    own_rows = lax.all_gather(tokens, "expert", axis=0, tiled=True)
    rows = lax.all_gather(own_rows, "mp", axis=1, tiled=True)
    row_count = rows.shape[0]
    adapter_of = token_adapters(request_lengths, request_adapter, request_order, row_count)
    rank_w = adapter_in[0]
    rank_cols = contract_last(rows, rank_w)
    per_device = rank_w.shape[0] // RANK
    local_adapter = adapter_of - lax.axis_index("mp") * per_device
    local_pick = (
        local_adapter[:, None] == jnp.arange(per_device, dtype=jnp.int32)[None, :]
    ).astype(jnp.float32)
    rank_part = jnp.sum(
        rank_cols.reshape(row_count, per_device, RANK) * local_pick[:, :, None], axis=1
    )
    rank = lax.psum(rank_part.astype(jnp.bfloat16), "mp")
    gate_pre = contract_last(rows, gate_weight[0])
    up_base = contract_last(rows, up_weight[0])
    chosen = (adapter_of[:, None] == jnp.arange(ADAPTERS, dtype=jnp.int32)[None, :]).astype(
        jnp.bfloat16
    )
    expanded = (rank[:, None, :] * chosen[:, :, None]).reshape(row_count, ADAPTERS * RANK)
    up = up_base + contract_last(expanded, adapter_out[0])
    hidden = (jax.nn.silu(gate_pre) * up).astype(jnp.bfloat16)
    partial = jnp.dot(hidden, down_weight[0], preferred_element_type=jnp.float32)
    mine = lax.psum_scatter(
        partial.astype(jnp.bfloat16), "mp", scatter_dimension=1, tiled=True
    )
    back = lax.all_to_all(
        mine.reshape(groups, tok_rows, cols), "expert", split_axis=0, concat_axis=0, tiled=True
    )
    expert_ids = jnp.arange(groups, dtype=jnp.int32)
    weights = jnp.sum(
        jnp.where(expert_route[:, :, None] == expert_ids, route_gate[:, :, None], 0.0), axis=1
    )
    mixed = jnp.sum(weights.T[:, :, None] * back.astype(jnp.float32), axis=0)
    return mixed.astype(jnp.bfloat16)


def xor4(a, b):
    return (a + b) % 2 + 2 * ((a // 2 + b // 2) % 2)


def kernel(
    len_ref,
    req_adapter_ref,
    order_ref,
    tok_ref,
    route_ref,
    weigh_ref,
    gw_hbm,
    uw_hbm,
    dw_hbm,
    ain_hbm,
    aout_hbm,
    out_ref,
    gw,
    uw,
    dw,
    ain,
    aout,
    x_buf,
    part,
    pair_in,
    pair_sum,
    quad_in,
    e_buf,
    back,
    rk_buf,
    adp,
    g_ref,
    exp_ref,
    h_ref,
    w_sem,
    loc_sem,
    z_send,
    z_recv,
    xy_send,
    xy_recv,
    dg_send,
    dg_recv,
    sib_send,
    sib_recv,
    rk_send,
    rk_recv,
    r1_send,
    r1_recv,
    r2_send,
    r2_recv,
    e_send,
    e_recv,
):
    T, C = tok_ref.shape
    H = T // 2
    z = lax.axis_index("expert")
    m = lax.axis_index("mp")
    q = m // 2
    c = m % 2
    sibling = (z, 2 * q + 1 - c)

    def chip(j):
        return xor4(q, j)

    def col(index):
        return pl.ds(pl.multiple_of(index * C, C), C)

    def remote(src, dst, send, recv, target):
        return pltpu.make_async_remote_copy(
            src_ref=src, dst_ref=dst, send_sem=send, recv_sem=recv,
            device_id=target, device_id_type=MESH,
        )

    def z_copy(s):
        return remote(
            x_buf.at[0, :, col(m)], x_buf.at[s, :, col(m)],
            z_send.at[s], z_recv.at[s], (xor4(z, s), m),
        )

    def xy_copy(s, j):
        ref = x_buf.at[s, :, col(m)]
        return remote(ref, ref, xy_send.at[s, j], xy_recv.at[s, j], (z, 2 * chip(j) + c))

    def dg_copy(s, j):
        ref = x_buf.at[s, pl.ds(H * (j - 1), H), col(2 * chip(j) + c)]
        return remote(
            ref, ref, dg_send.at[s, j], dg_recv.at[s, j], (z, 2 * chip(3 - j) + c)
        )

    def sib_copy(s, j):
        ref = x_buf.at[s, :, col(2 * chip(j) + c)]
        return remote(ref, ref, sib_send.at[s, j], sib_recv.at[s, j], sibling)

    def rk_copy(s, d):
        return remote(
            rk_buf.at[s, 0], rk_buf.at[s, d],
            rk_send.at[s, d], rk_recv.at[s, d], (z, (m + d) % 8),
        )

    def r1_copy(s, j):
        return remote(
            part.at[s, :, col(2 * j + 1 - c)], pair_in.at[s, :, pl.ds(j * C, C)],
            r1_send.at[s, j], r1_recv.at[s, j], sibling,
        )

    def r2_copy(s, j):
        return remote(
            pair_sum.at[s, :, col(chip(j))], quad_in.at[s, j],
            r2_send.at[s, j], r2_recv.at[s, j], (z, 2 * chip(j) + c),
        )

    def e_copy(s):
        return remote(e_buf.at[s], back.at[s], e_send.at[s], e_recv.at[s], (xor4(z, s), m))

    first = pltpu.make_async_copy(tok_ref, x_buf.at[0, :, col(m)], loc_sem)
    first.start()
    weights = [
        pltpu.make_async_copy(src.at[0], dst, w_sem.at[i])
        for i, (src, dst) in enumerate(
            ((ain_hbm, ain), (gw_hbm, gw), (uw_hbm, uw), (aout_hbm, aout), (dw_hbm, dw))
        )
    ]
    for copy in weights:
        copy.start()

    barrier = pltpu.get_barrier_semaphore()
    for s in range(1, 4):
        pl.semaphore_signal(barrier, inc=1, device_id=(xor4(z, s), m), device_id_type=MESH)
    for d in range(1, 8):
        pl.semaphore_signal(barrier, inc=1, device_id=(z, (m + d) % 8), device_id_type=MESH)
    pl.semaphore_wait(barrier, 10)

    first.wait()

    def begin(s):
        for j in (1, 2):
            xy_copy(s, j).start()
        sib_copy(s, 0).start()

    def forward(s):
        for j in (1, 2):
            xy_copy(s, j).wait_recv()
            dg_copy(s, j).start()
            sib_copy(s, j).start()

    def finish(s):
        for j in (1, 2):
            dg_copy(s, j).wait_recv()
        sib_copy(s, 3).start()
        for j in range(4):
            sib_copy(s, j).wait_recv()

    z_copy(1).start()
    begin(0)
    z_copy(2).start()
    z_copy(3).start()

    start = jnp.int32(0)
    starts, ids = [], []
    for j in range(len_ref.shape[0]):
        request = order_ref[j]
        starts.append(start)
        ids.append(req_adapter_ref[request])
        start = start + len_ref[request]
    for s in range(4):
        position = xor4(z, s) * T + lax.broadcasted_iota(jnp.int32, (1, T), 1)
        value = jnp.zeros((1, T), jnp.int32)
        for at, adapter in zip(starts, ids):
            value = jnp.where(position >= at, adapter, value)
        adp[s] = value

    forward(0)
    for copy in weights:
        copy.wait()

    def quad_finish(s):
        for j in range(1, 4):
            r2_copy(s, j).wait_recv()
        total = pair_sum[s, :, col(q)].astype(jnp.float32)
        for j in range(1, 4):
            total = total + quad_in[s, j].astype(jnp.float32)
        e_buf[s] = total.astype(jnp.bfloat16)

    per_device = ain.shape[0] // RANK

    def step(s, carry):
        @pl.when(s < 3)
        def _():
            z_copy(s + 1).wait_recv()
            begin(s + 1)

        finish(s)
        adapter_row = adp[s]
        rank_cols = contract_last(ain[...], x_buf[s])
        group = lax.broadcasted_iota(jnp.int32, rank_cols.shape, 0) // RANK + per_device * m
        picked = jnp.where(group == adapter_row, rank_cols, 0.0)
        total = picked[0:RANK]
        for g in range(1, per_device):
            total = total + picked[g * RANK : (g + 1) * RANK]
        rk_buf[s, 0] = total.astype(jnp.bfloat16)
        for d in range(1, 8):
            rk_copy(s, d).start()

        g_ref[...] = contract_last(x_buf[s], gw[...])

        @pl.when(s < 3)
        def _():
            forward(s + 1)

        up_base = contract_last(x_buf[s], uw[...])
        for d in range(1, 8):
            rk_copy(s, d).wait_recv()
        rank = rk_buf[s, 0].astype(jnp.float32)
        for d in range(1, 8):
            rank = rank + rk_buf[s, d].astype(jnp.float32)
        rank_cols8 = jnp.concatenate([rank] * 8, axis=0).T
        adapter_cols = jnp.broadcast_to(adapter_row.astype(jnp.float32), (128, T)).T
        lane_group = (lax.broadcasted_iota(jnp.int32, (T, 128), 1) // RANK).astype(jnp.float32)
        for g in range(ADAPTERS // 8):
            exp_ref[:, g * 128 : (g + 1) * 128] = jnp.where(
                lane_group + 8.0 * g == adapter_cols, rank_cols8, 0.0
            ).astype(jnp.bfloat16)
        up = up_base + contract_last(exp_ref[...], aout[...])
        gate = g_ref[...]
        h_ref[...] = (jax.nn.silu(gate) * up).astype(jnp.bfloat16)
        width = 2 * C
        for j in range(4):
            part[s, :, j * width : (j + 1) * width] = jnp.dot(
                h_ref[...], dw[:, j * width : (j + 1) * width],
                preferred_element_type=jnp.float32,
            ).astype(jnp.bfloat16)
            r1_copy(s, j).start()

        @pl.when(s > 0)
        def _():
            quad_finish(s - 1)

        @pl.when(s > 1)
        def _():
            e_copy(s - 1).start()

        for j in range(4):
            r1_copy(s, j).wait_recv()
            pair_sum[s, :, j * C : (j + 1) * C] = (
                part[s, :, col(2 * j + c)].astype(jnp.float32)
                + pair_in[s, :, j * C : (j + 1) * C].astype(jnp.float32)
            ).astype(jnp.bfloat16)
        for j in (3, 1, 2):
            r2_copy(s, j).start()
        return carry

    lax.fori_loop(0, 4, step, 0)
    quad_finish(3)
    e_copy(3).start()

    def weight_of(s):
        hit = route_ref[...] == xor4(z, s)
        return jnp.sum(jnp.where(hit, weigh_ref[...], 0.0), axis=1, keepdims=True)

    mixed = weight_of(0) * e_buf[0].astype(jnp.float32)
    for s in range(1, 4):
        e_copy(s).wait_recv()
        mixed = mixed + weight_of(s) * back[s].astype(jnp.float32)
    out_ref[...] = mixed.astype(jnp.bfloat16)

    for s in range(1, 4):
        z_copy(s).wait_send()
        e_copy(s).wait_send()

    def drain(s, carry):
        for j in (1, 2):
            xy_copy(s, j).wait_send()
            dg_copy(s, j).wait_send()
        for j in range(4):
            sib_copy(s, j).wait_send()
            r1_copy(s, j).wait_send()
        for j in range(1, 4):
            r2_copy(s, j).wait_send()
        for d in range(1, 8):
            rk_copy(s, d).wait_send()
        return carry

    lax.fori_loop(0, 4, drain, 0)


def fused(
    tokens,
    expert_route,
    route_gate,
    request_lengths,
    request_adapter,
    request_order,
    gate_weight,
    up_weight,
    down_weight,
    adapter_in,
    adapter_out,
):
    T, C = tokens.shape
    D = gate_weight.shape[2]
    F = gate_weight.shape[1]
    A = adapter_in.shape[1]
    bf16 = jnp.bfloat16
    dma = pltpu.SemaphoreType.DMA
    vmem = pl.BlockSpec(memory_space=pltpu.VMEM)
    smem = pl.BlockSpec(memory_space=pltpu.SMEM)
    hbm = pl.BlockSpec(memory_space=pl.ANY)
    return pl.pallas_call(
        kernel,
        out_shape=jax.ShapeDtypeStruct((T, C), bf16),
        in_specs=[smem, smem, smem, hbm, vmem, vmem, hbm, hbm, hbm, hbm, hbm],
        out_specs=vmem,
        scratch_shapes=[
            pltpu.VMEM((F, D), bf16),
            pltpu.VMEM((F, D), bf16),
            pltpu.VMEM((F, D), bf16),
            pltpu.VMEM((A, D), bf16),
            pltpu.VMEM((F, ADAPTERS * RANK), bf16),
            pltpu.VMEM((4, T, D), bf16),
            pltpu.VMEM((4, T, D), bf16),
            pltpu.VMEM((4, T, 4 * C), bf16),
            pltpu.VMEM((4, T, 4 * C), bf16),
            pltpu.VMEM((4, 4, T, C), bf16),
            pltpu.VMEM((4, T, C), bf16),
            pltpu.VMEM((4, T, C), bf16),
            pltpu.VMEM((4, 8, RANK, T), bf16),
            pltpu.VMEM((4, 1, T), jnp.int32),
            pltpu.VMEM((T, F), jnp.float32),
            pltpu.VMEM((T, ADAPTERS * RANK), bf16),
            pltpu.VMEM((T, F), bf16),
            dma((5,)),
            dma,
            dma((4,)),
            dma((4,)),
            dma((4, 4)),
            dma((4, 4)),
            dma((4, 4)),
            dma((4, 4)),
            dma((4, 4)),
            dma((4, 4)),
            dma((4, 8)),
            dma((4, 8)),
            dma((4, 4)),
            dma((4, 4)),
            dma((4, 4)),
            dma((4, 4)),
            dma((4,)),
            dma((4,)),
        ],
        compiler_params=pltpu.CompilerParams(
            collective_id=0, has_side_effects=True, vmem_limit_bytes=60 * 1024 * 1024
        ),
        cost_estimate=pl.CostEstimate(
            flops=8 * T * (3 * F * D + A * D + F * ADAPTERS * RANK),
            bytes_accessed=2 * (3 * F * D + A * D + F * ADAPTERS * RANK),
            transcendentals=4 * T * F,
        ),
    )(
        request_lengths,
        request_adapter,
        request_order,
        tokens,
        expert_route,
        route_gate,
        gate_weight,
        up_weight,
        down_weight,
        adapter_in,
        adapter_out,
    )


def solution(mesh):
    in_specs = (
        P("expert", "mp"),
        P("expert", None),
        P("expert", None),
        P(),
        P(),
        P(),
        P("expert", "mp", None),
        P("expert", "mp", None),
        P("expert", "mp", None),
        P("expert", "mp", None),
        P("expert", "mp", None),
    )
    out_specs = P("expert", "mp")
    small = mesh.shape["expert"] == 4 and mesh.shape["mp"] == 8
    return jax.shard_map(
        fused if small else plain,
        mesh=mesh, in_specs=in_specs, out_specs=out_specs, check_vma=False,
    )
```

time: 457 us -> 146 us (0.32)
  waiting for transfers between devices: 310 us -> 0 us
  Pallas kernels: 0 us -> 141 us
  local copies, waits for them, and re-layouts: 51.3 us -> 4.74 us
  matrix products: 45.2 us -> 0 us
  other arithmetic: 20.1 us -> 0 us
  starting transfers between devices: 16.8 us -> 0 us
  between operations: 13.3 us -> 0.01 us
    all_to_all x3 -> x0, waiting for transfers between devices: 208 us -> none  [the longest x1 183 us: on_device(): lax.all_to_all(send_rows, 'expert', split_axis=0, concat_axis=0, tiled=True)]
    pallas_call x0 -> x1, Pallas kernels: none -> 141 us  [fused(): pl.pallas_call(kernel, out_shape=jax.ShapeDtypeStruct((T, C), bf16), in_s...]
    reduce_scatter x1 -> x0, waiting for transfers between devices: 70.9 us -> none  [on_device(): lax.psum_scatter(lax.dot_general(down_w, hidden, (((0,), (1,)), ((), ()))...]
    dot_general x4 -> x0, matrix products: 45.2 us -> none  [the longest x3 28.3 us: contract_last(): lax.dot_general(left, right, (((1,), (1,)), ((), ())), preferred_element_...]
    gather x3 -> x0, local copies, waits for them, and re-layouts: 36.2 us -> none  [the longest x1 18.2 us: on_device(): send_rows = jnp.where(filled[:, None], full_rows[slot_token], blank)]
    psum x1 -> x0, waiting for transfers between devices: 30.2 us -> none  [on_device(): rank = lax.psum(rank_part.astype(jnp.bfloat16), 'mp')]
    all_to_all x3 -> x0, starting transfers between devices: 16.6 us -> none  [the longest x1 6.32 us: on_device(): lax.all_to_all(slot_adapter, 'expert', split_axis=0, concat_axis=0, tiled...]
    select_n x4 -> x0, other arithmetic: 9.55 us -> none  [the longest x1 7.25 us: on_device(): send_rows = jnp.where(filled[:, None], full_rows[slot_token], blank)]
  transfers between devices with their start and end apart: 6 -> 0, of which waited for: 4 -> 0; matrix products, arithmetic and copies ran while one was open for 17% -> 0% of each run, Pallas kernels for 0% -> 0%
where the time goes in v1:
time: 146 us
  Pallas kernels  141 us (97%)
  local copies, waits for them, and re-layouts  4.74 us (3%)
    pallas_call x1, Pallas kernels, fused(): pl.pallas_call(kernel, out_shape=jax.ShapeDtypeStruct((T, C), bf16), in_s...  141 us
    unnamed x3, local copies, waits for them, and re-layouts  4.74 us

profile of v1, /device:TPU:0, one launch (start us, length us, event | category | flops | bytes accessed | tf_op | source)
XLA Modules:
  0.0 145.8 jit_solution(13623504691481969621)
XLA Ops:
  0.0 1.5 %copy.12.route_ref = s32[512,2]{1,0:T(8,128)} copy(s32[512,2]{0,1:T(2,128)} %param.12) | data formatting | bytes 8192 | tf_op args[1]
  1.5 1.5 %copy.13.weigh_ref = f32[512,2]{1,0:T(8,128)} copy(f32[512,2]{0,1:T(2,128)} %param.13) | data formatting | bytes 8192 | tf_op args[2]
  3.1 141.0 %shard_map.109 = bf16[512,256]{1,0:T(8,128)(2,1)} custom-call(s32[16]{0:T(128)} %len_ref.1, s32[16]{0:T(128)} %req_adapter_ref.1, s32[16]{0:T(128)} %order_ref.1, bf16[512,256]{1,0:T(8,128)(2,1)} %tok_ref.1, s32[512,2]{1,0:T(8,128)} %copy.12.route_ref, f32[512,2]{1,0:T(8,128)} %copy.13.weigh_ref, bf16[1,704,2048]{2,1,0:T(8,128)(2,1)} %gw_hbm.1, ...), custom_call_target="tpu_custom_call" | custom-call | flops 21743271936 | bytes 10616832 | tf_op jit(solution)/shard_map/pallas_call | solution.py:395
  144.1 1.7 %copy.15 = bf16[512,256]{1,0:T(8,128)(2,1)} copy(bf16[512,256]{1,0:T(8,128)(2,1)} %shard_map.109) | data formatting | bytes 524288

commit v2 on v1

--- a/solution.py
+++ b/solution.py
@@ -87,6 +87,10 @@
 
 def xor4(a, b):
     return (a + b) % 2 + 2 * ((a // 2 + b // 2) % 2)
+
+
+def mask_of(s):
+    return s // 2 + 2 * (((s + 1) // 2) % 2)
 
 
 def kernel(
@@ -119,6 +123,7 @@
     g_ref,
     exp_ref,
     h_ref,
+    w_cols,
     w_sem,
     loc_sem,
     z_send,
@@ -135,6 +140,8 @@
     r1_recv,
     r2_send,
     r2_recv,
+    n_send,
+    n_recv,
     e_send,
     e_recv,
 ):
@@ -161,7 +168,7 @@
     def z_copy(s):
         return remote(
             x_buf.at[0, :, col(m)], x_buf.at[s, :, col(m)],
-            z_send.at[s], z_recv.at[s], (xor4(z, s), m),
+            z_send.at[s], z_recv.at[s], (xor4(z, mask_of(s)), m),
         )
 
     def xy_copy(s, j):
@@ -186,18 +193,28 @@
 
     def r1_copy(s, j):
         return remote(
-            part.at[s, :, col(2 * j + 1 - c)], pair_in.at[s, :, pl.ds(j * C, C)],
+            part.at[s, :, col(2 * chip(j) + 1 - c)], pair_in.at[s, :, col(chip(j))],
             r1_send.at[s, j], r1_recv.at[s, j], sibling,
         )
 
-    def r2_copy(s, j):
+    def half(h):
+        return pl.ds(H * h, H)
+
+    def d_copy(s, j):
         return remote(
-            pair_sum.at[s, :, col(chip(j))], quad_in.at[s, j],
+            pair_sum.at[s, half(j - 1), col(chip(3))], quad_in.at[s, 3, half(j - 1)],
             r2_send.at[s, j], r2_recv.at[s, j], (z, 2 * chip(j) + c),
         )
 
+    def n_copy(s, j, h):
+        i = 2 * (j - 1) + h
+        return remote(
+            pair_sum.at[s, half(h), col(chip(j))], quad_in.at[s, j, half(h)],
+            n_send.at[s, i], n_recv.at[s, i], (z, 2 * chip(j) + c),
+        )
+
     def e_copy(s):
-        return remote(e_buf.at[s], back.at[s], e_send.at[s], e_recv.at[s], (xor4(z, s), m))
+        return remote(e_buf.at[s], back.at[s], e_send.at[s], e_recv.at[s], (xor4(z, mask_of(s)), m))
 
     first = pltpu.make_async_copy(tok_ref, x_buf.at[0, :, col(m)], loc_sem)
     first.start()
@@ -212,7 +229,7 @@
 
     barrier = pltpu.get_barrier_semaphore()
     for s in range(1, 4):
-        pl.semaphore_signal(barrier, inc=1, device_id=(xor4(z, s), m), device_id_type=MESH)
+        pl.semaphore_signal(barrier, inc=1, device_id=(xor4(z, mask_of(s)), m), device_id_type=MESH)
     for d in range(1, 8):
         pl.semaphore_signal(barrier, inc=1, device_id=(z, (m + d) % 8), device_id_type=MESH)
     pl.semaphore_wait(barrier, 10)
@@ -239,8 +256,6 @@
 
     z_copy(1).start()
     begin(0)
-    z_copy(2).start()
-    z_copy(3).start()
 
     start = jnp.int32(0)
     starts, ids = [], []
@@ -250,23 +265,47 @@
         ids.append(req_adapter_ref[request])
         start = start + len_ref[request]
     for s in range(4):
-        position = xor4(z, s) * T + lax.broadcasted_iota(jnp.int32, (1, T), 1)
+        position = xor4(z, mask_of(s)) * T + lax.broadcasted_iota(jnp.int32, (1, T), 1)
         value = jnp.zeros((1, T), jnp.int32)
         for at, adapter in zip(starts, ids):
             value = jnp.where(position >= at, adapter, value)
         adp[s] = value
 
+    hits = [
+        jnp.sum(
+            jnp.where(route_ref[...] == xor4(z, mask_of(s)), weigh_ref[...], 0.0),
+            axis=0, keepdims=True,
+        )
+        for s in range(4)
+    ]
+    w_cols[...] = jnp.concatenate(hits + [jnp.zeros((124, T), jnp.float32)], axis=0).T
+
     forward(0)
+    z_copy(2).start()
+    z_copy(3).start()
     for copy in weights:
         copy.wait()
 
+    def quad_middle(s):
+        for j in (1, 2):
+            h = j - 1
+            d_copy(s, j).wait_recv()
+            where = col(chip(3 - j))
+            pair_sum[s, half(h), where] = (
+                pair_sum[s, half(h), where].astype(jnp.float32)
+                + quad_in[s, 3, half(h)].astype(jnp.float32)
+            ).astype(jnp.bfloat16)
+            n_copy(s, 3 - j, h).start()
+
     def quad_finish(s):
-        for j in range(1, 4):
-            r2_copy(s, j).wait_recv()
-        total = pair_sum[s, :, col(q)].astype(jnp.float32)
-        for j in range(1, 4):
-            total = total + quad_in[s, j].astype(jnp.float32)
-        e_buf[s] = total.astype(jnp.bfloat16)
+        for j in (1, 2):
+            for h in range(2):
+                n_copy(s, j, h).wait_recv()
+        e_buf[s] = (
+            pair_sum[s, :, col(q)].astype(jnp.float32)
+            + quad_in[s, 1].astype(jnp.float32)
+            + quad_in[s, 2].astype(jnp.float32)
+        ).astype(jnp.bfloat16)
 
     per_device = ain.shape[0] // RANK
 
@@ -289,6 +328,10 @@
             rk_copy(s, d).start()
 
         g_ref[...] = contract_last(x_buf[s], gw[...])
+
+        @pl.when(s > 0)
+        def _():
+            quad_middle(s - 1)
 
         @pl.when(s < 3)
         def _():
@@ -310,13 +353,34 @@
         up = up_base + contract_last(exp_ref[...], aout[...])
         gate = g_ref[...]
         h_ref[...] = (jax.nn.silu(gate) * up).astype(jnp.bfloat16)
-        width = 2 * C
-        for j in range(4):
-            part[s, :, j * width : (j + 1) * width] = jnp.dot(
-                h_ref[...], dw[:, j * width : (j + 1) * width],
-                preferred_element_type=jnp.float32,
+
+        def down(j):
+            block = pl.ds(pl.multiple_of(chip(j) * 2 * C, 2 * C), 2 * C)
+            part[s, :, block] = jnp.dot(
+                h_ref[...], dw[:, block], preferred_element_type=jnp.float32
             ).astype(jnp.bfloat16)
             r1_copy(s, j).start()
+
+        def pair(j):
+            r1_copy(s, j).wait_recv()
+            where = col(chip(j))
+            pair_sum[s, :, where] = (
+                part[s, :, col(2 * chip(j) + c)].astype(jnp.float32)
+                + pair_in[s, :, where].astype(jnp.float32)
+            ).astype(jnp.bfloat16)
+
+        down(3)
+        down(1)
+        pair(3)
+        d_copy(s, 1).start()
+        d_copy(s, 2).start()
+        down(2)
+        pair(1)
+        n_copy(s, 1, 0).start()
+        down(0)
+        pair(2)
+        n_copy(s, 2, 1).start()
+        pair(0)
 
         @pl.when(s > 0)
         def _():
@@ -326,28 +390,17 @@
         def _():
             e_copy(s - 1).start()
 
-        for j in range(4):
-            r1_copy(s, j).wait_recv()
-            pair_sum[s, :, j * C : (j + 1) * C] = (
-                part[s, :, col(2 * j + c)].astype(jnp.float32)
-                + pair_in[s, :, j * C : (j + 1) * C].astype(jnp.float32)
-            ).astype(jnp.bfloat16)
-        for j in (3, 1, 2):
-            r2_copy(s, j).start()
         return carry
 
     lax.fori_loop(0, 4, step, 0)
+    quad_middle(3)
     quad_finish(3)
     e_copy(3).start()
 
-    def weight_of(s):
-        hit = route_ref[...] == xor4(z, s)
-        return jnp.sum(jnp.where(hit, weigh_ref[...], 0.0), axis=1, keepdims=True)
-
-    mixed = weight_of(0) * e_buf[0].astype(jnp.float32)
+    mixed = w_cols[:, 0:1] * e_buf[0].astype(jnp.float32)
     for s in range(1, 4):
         e_copy(s).wait_recv()
-        mixed = mixed + weight_of(s) * back[s].astype(jnp.float32)
+        mixed = mixed + w_cols[:, s : s + 1] * back[s].astype(jnp.float32)
     out_ref[...] = mixed.astype(jnp.bfloat16)
 
     for s in range(1, 4):
@@ -361,8 +414,10 @@
         for j in range(4):
             sib_copy(s, j).wait_send()
             r1_copy(s, j).wait_send()
-        for j in range(1, 4):
-            r2_copy(s, j).wait_send()
+        for j in (1, 2):
+            d_copy(s, j).wait_send()
+            for h in range(2):
+                n_copy(s, j, h).wait_send()
         for d in range(1, 8):
             rk_copy(s, d).wait_send()
         return carry
@@ -415,6 +470,7 @@
             pltpu.VMEM((T, F), jnp.float32),
             pltpu.VMEM((T, ADAPTERS * RANK), bf16),
             pltpu.VMEM((T, F), bf16),
+            pltpu.VMEM((T, 128), jnp.float32),
             dma((5,)),
             dma,
             dma((4,)),
@@ -427,6 +483,8 @@
             dma((4, 4)),
             dma((4, 8)),
             dma((4, 8)),
+            dma((4, 4)),
+            dma((4, 4)),
             dma((4, 4)),
             dma((4, 4)),
             dma((4, 4)),
@@ -447,8 +505,8 @@
         request_adapter,
         request_order,
         tokens,
-        expert_route,
-        route_gate,
+        expert_route.T,
+        route_gate.T,
         gate_weight,
         up_weight,
         down_weight,

time: 146 us -> 120 us (0.82)
  Pallas kernels: 141 us -> 118 us
  local copies, waits for them, and re-layouts: 4.74 us -> 1.67 us
    pallas_call x1, Pallas kernels: 141 us -> 118 us  [fused(): pl.pallas_call(kernel, out_shape=jax.ShapeDtypeStruct((T, C), bf16), in_s...]
    unnamed x3 -> x1, local copies, waits for them, and re-layouts: 4.74 us -> 1.67 us
where the time goes in v2:
time: 120 us; the launch traced here: 119 us
  Pallas kernels  118 us (98%)
  local copies, waits for them, and re-layouts  1.67 us (1%)
    pallas_call x1, Pallas kernels, fused(): pl.pallas_call(kernel, out_shape=jax.ShapeDtypeStruct((T, C), bf16), in_s...  118 us

profile of v2, /device:TPU:0, one launch (start us, length us, event | category | flops | bytes accessed | tf_op | source)
XLA Modules:
  0.0 119.4 jit_solution(6434702712279517386)
XLA Ops:
  0.0 117.7 %shard_map.109 = bf16[512,256]{1,0:T(8,128)(2,1)} custom-call(s32[16]{0:T(128)} %len_ref.1, s32[16]{0:T(128)} %req_adapter_ref.1, s32[16]{0:T(128)} %order_ref.1, bf16[512,256]{1,0:T(8,128)(2,1)} %tok_ref.1, s32[2,512]{1,0:T(2,128)} %bitcast.2, f32[2,512]{1,0:T(2,128)} %bitcast.3, bf16[1,704,2048]{2,1,0:T(8,128)(2,1)} %gw_hbm.1, ...), custom_call_target="tpu_custom_call" | custom-call | flops 21743271936 | bytes 10616832 | tf_op jit(solution)/shard_map/pallas_call | solution.py:450
  117.7 1.7 %copy.13 = bf16[512,256]{1,0:T(8,128)(2,1)} copy(bf16[512,256]{1,0:T(8,128)(2,1)} %shard_map.109) | data formatting | bytes 524288

commit v3 on v2

--- a/solution.py
+++ b/solution.py
@@ -121,6 +121,7 @@
     rk_buf,
     adp,
     g_ref,
+    u_ref,
     exp_ref,
     h_ref,
     w_cols,
@@ -247,10 +248,12 @@
             dg_copy(s, j).start()
             sib_copy(s, j).start()
 
-    def finish(s):
+    def late(s):
         for j in (1, 2):
             dg_copy(s, j).wait_recv()
         sib_copy(s, 3).start()
+
+    def finish(s):
         for j in range(4):
             sib_copy(s, j).wait_recv()
 
@@ -283,6 +286,9 @@
     forward(0)
     z_copy(2).start()
     z_copy(3).start()
+    z_copy(1).wait_recv()
+    begin(1)
+    late(0)
     for copy in weights:
         copy.wait()
 
@@ -309,17 +315,10 @@
 
     per_device = ain.shape[0] // RANK
 
-    def step(s, carry):
-        @pl.when(s < 3)
-        def _():
-            z_copy(s + 1).wait_recv()
-            begin(s + 1)
-
-        finish(s)
-        adapter_row = adp[s]
+    def send_rank(s):
         rank_cols = contract_last(ain[...], x_buf[s])
         group = lax.broadcasted_iota(jnp.int32, rank_cols.shape, 0) // RANK + per_device * m
-        picked = jnp.where(group == adapter_row, rank_cols, 0.0)
+        picked = jnp.where(group == adp[s], rank_cols, 0.0)
         total = picked[0:RANK]
         for g in range(1, per_device):
             total = total + picked[g * RANK : (g + 1) * RANK]
@@ -327,17 +326,23 @@
         for d in range(1, 8):
             rk_copy(s, d).start()
 
-        g_ref[...] = contract_last(x_buf[s], gw[...])
-
-        @pl.when(s > 0)
-        def _():
-            quad_middle(s - 1)
+    finish(0)
+    send_rank(0)
+    g_ref[...] = contract_last(x_buf[0], gw[...])
+    forward(1)
+    u_ref[...] = contract_last(x_buf[0], uw[...])
+
+    def step(s, carry):
+        @pl.when(s < 2)
+        def _():
+            z_copy(s + 2).wait_recv()
+            begin(s + 2)
 
         @pl.when(s < 3)
         def _():
-            forward(s + 1)
-
-        up_base = contract_last(x_buf[s], uw[...])
+            late(s + 1)
+
+        adapter_row = adp[s]
         for d in range(1, 8):
             rk_copy(s, d).wait_recv()
         rank = rk_buf[s, 0].astype(jnp.float32)
@@ -350,9 +355,14 @@
             exp_ref[:, g * 128 : (g + 1) * 128] = jnp.where(
                 lane_group + 8.0 * g == adapter_cols, rank_cols8, 0.0
             ).astype(jnp.bfloat16)
-        up = up_base + contract_last(exp_ref[...], aout[...])
+        up = u_ref[...] + contract_last(exp_ref[...], aout[...])
         gate = g_ref[...]
         h_ref[...] = (jax.nn.silu(gate) * up).astype(jnp.bfloat16)
+
+        @pl.when(s < 3)
+        def _():
+            finish(s + 1)
+            send_rank(s + 1)
 
         def down(j):
             block = pl.ds(pl.multiple_of(chip(j) * 2 * C, 2 * C), 2 * C)
@@ -390,10 +400,23 @@
         def _():
             e_copy(s - 1).start()
 
+        @pl.when(s < 2)
+        def _():
+            forward(s + 2)
+
+        @pl.when(s < 3)
+        def _():
+            g_ref[...] = contract_last(x_buf[s + 1], gw[...])
+
+        quad_middle(s)
+
+        @pl.when(s < 3)
+        def _():
+            u_ref[...] = contract_last(x_buf[s + 1], uw[...])
+
         return carry
 
     lax.fori_loop(0, 4, step, 0)
-    quad_middle(3)
     quad_finish(3)
     e_copy(3).start()
 
@@ -468,6 +491,7 @@
             pltpu.VMEM((4, 8, RANK, T), bf16),
             pltpu.VMEM((4, 1, T), jnp.int32),
             pltpu.VMEM((T, F), jnp.float32),
+            pltpu.VMEM((T, F), jnp.float32),
             pltpu.VMEM((T, ADAPTERS * RANK), bf16),
             pltpu.VMEM((T, F), bf16),
             pltpu.VMEM((T, 128), jnp.float32),

time: 120 us -> 110 us (0.917)
  Pallas kernels: 118 us -> 108 us
    pallas_call x1, Pallas kernels: 118 us -> 108 us  [fused(): pl.pallas_call(kernel, out_shape=jax.ShapeDtypeStruct((T, C), bf16), in_s...]
where the time goes in v3:
time: 110 us
  Pallas kernels  108 us (98%)
  local copies, waits for them, and re-layouts  1.67 us (2%)
    pallas_call x1, Pallas kernels, fused(): pl.pallas_call(kernel, out_shape=jax.ShapeDtypeStruct((T, C), bf16), in_s...  108 us

profile of v3, /device:TPU:0, one launch (start us, length us, event | category | flops | bytes accessed | tf_op | source)
XLA Modules:
  0.0 110.1 jit_solution(5906638841998352632)
XLA Ops:
  0.0 108.4 %shard_map.109 = bf16[512,256]{1,0:T(8,128)(2,1)} custom-call(s32[16]{0:T(128)} %len_ref.1, s32[16]{0:T(128)} %req_adapter_ref.1, s32[16]{0:T(128)} %order_ref.1, bf16[512,256]{1,0:T(8,128)(2,1)} %tok_ref.1, s32[2,512]{1,0:T(2,128)} %bitcast.2, f32[2,512]{1,0:T(2,128)} %bitcast.3, bf16[1,704,2048]{2,1,0:T(8,128)(2,1)} %gw_hbm.1, ...), custom_call_target="tpu_custom_call" | custom-call | flops 21743271936 | bytes 10616832 | tf_op jit(solution)/shard_map/pallas_call | solution.py:473
  108.4 1.7 %copy.13 = bf16[512,256]{1,0:T(8,128)(2,1)} copy(bf16[512,256]{1,0:T(8,128)(2,1)} %shard_map.109) | data formatting | bytes 524288

commit v4 on v3

--- a/solution.py
+++ b/solution.py
@@ -384,6 +384,15 @@
         pair(3)
         d_copy(s, 1).start()
         d_copy(s, 2).start()
+
+        @pl.when(s > 0)
+        def _():
+            quad_finish(s - 1)
+
+        @pl.when(s > 1)
+        def _():
+            e_copy(s - 1).start()
+
         down(2)
         pair(1)
         n_copy(s, 1, 0).start()
@@ -391,14 +400,6 @@
         pair(2)
         n_copy(s, 2, 1).start()
         pair(0)
-
-        @pl.when(s > 0)
-        def _():
-            quad_finish(s - 1)
-
-        @pl.when(s > 1)
-        def _():
-            e_copy(s - 1).start()
 
         @pl.when(s < 2)
         def _():

time: 110 us -> 110 us (level)
  no operation moved by 1% of the time
where the time goes in v4:
time: 110 us; the launch traced here: 109 us
  Pallas kernels  108 us (98%)
  local copies, waits for them, and re-layouts  1.67 us (2%)
    pallas_call x1, Pallas kernels, fused(): pl.pallas_call(kernel, out_shape=jax.ShapeDtypeStruct((T, C), bf16), in_s...  108 us

profile of v4, /device:TPU:0, one launch (start us, length us, event | category | flops | bytes accessed | tf_op | source)
XLA Modules:
  0.0 109.4 jit_solution(8634754926482513072)
XLA Ops:
  0.0 107.7 %shard_map.109 = bf16[512,256]{1,0:T(8,128)(2,1)} custom-call(s32[16]{0:T(128)} %len_ref.1, s32[16]{0:T(128)} %req_adapter_ref.1, s32[16]{0:T(128)} %order_ref.1, bf16[512,256]{1,0:T(8,128)(2,1)} %tok_ref.1, s32[2,512]{1,0:T(2,128)} %bitcast.2, f32[2,512]{1,0:T(2,128)} %bitcast.3, bf16[1,704,2048]{2,1,0:T(8,128)(2,1)} %gw_hbm.1, ...), custom_call_target="tpu_custom_call" | custom-call | flops 21743271936 | bytes 10616832 | tf_op jit(solution)/shard_map/pallas_call | solution.py:474
  107.7 1.7 %copy.13 = bf16[512,256]{1,0:T(8,128)(2,1)} copy(bf16[512,256]{1,0:T(8,128)(2,1)} %shard_map.109) | data formatting | bytes 524288
